TPU v7x, 32 devices: a whole 2x2x4 slice. The times are simulated.
32 devices in a mesh: row: 2 (over core), col: 16 (over z, y, x).
Axes of the slice: x: 2, y: 2, z: 4, core: 2. Of those that a mesh axis runs over, the one named last changes fastest.
Arguments:
- node_latent: float32 [3072, 512], P(('row', 'col')), may hold values from -6 to 6
- edge_latent: bfloat16 [65536, 512], P(('row', 'col')), may hold values from -6 to 6
- senders: int32 [65536], P(('row', 'col')), may hold values from 0 to 3071, as said below
- receivers: int32 [65536], P(('row', 'col')), may hold values from 0 to 3071, as said below
- edge_count: int32 [32], P(('row', 'col')), may hold values from 512 to 2048, as said below
- edge_in: bfloat16 [2, 1536, 512], replicated, may hold values from -0.15625 to 0.15625
- edge_out: bfloat16 [2, 512, 512], replicated
- node_in: bfloat16 [2, 1024, 512], replicated, may hold values from -0.1875 to 0.1875
- node_out: bfloat16 [2, 512, 512], replicated
Outputs:
- updated_nodes: float32 [3072, 512], P(('row', 'col'))
Inputs may be any that keep to these rules, and one draw needn't show every extreme that they name: `senders`: the sender of every slot of tile t lies in sender patch t // 16. `receivers`: the receiver of every slot of tile t lies in receiver patch t % 16. Slots that are not live hold ids of the same patches. `edge_count`: some tile is full.
All inputs are finite; a program needn't handle non-finite values.
Results may differ from a plain program's by a relative error of at most 0.011.
Values may be sent and summed in bfloat16 or wider, within the bound.
A program may use at most 128 MiB of HBM per device.

v0:
```python
import jax
import jax.numpy as jnp
from jax import lax
from jax.sharding import PartitionSpec as P


def layer_norm(values):
    centre = values - jnp.mean(values, axis=-1, keepdims=True)
    spread = jnp.mean(centre * centre, axis=-1, keepdims=True)
    return centre * lax.rsqrt(spread + 1e-05)


def product(matrix, weight):
    return jnp.dot(matrix, weight, preferred_element_type=jnp.float32)


def node_section(latent, summed, w_first, w_second):
    joined = jnp.concatenate([latent.astype(jnp.bfloat16), summed.astype(jnp.bfloat16)], axis=1)
    hidden = jax.nn.silu(product(joined, w_first)).astype(jnp.bfloat16)
    return latent + layer_norm(product(hidden, w_second))


def per_device(
    node_latent, edge_latent, senders, receivers, edge_count, edge_in, edge_out, node_in, node_out
):
    own_rows = node_latent.shape[0]
    latent_width = node_latent.shape[1]
    slot_total = edge_latent.shape[0]
    layer_total = edge_in.shape[0]
    send_patch = own_rows * lax.axis_size("col")
    patch_rows = own_rows * lax.axis_size("row")
    row_index = lax.axis_index("row")
    send_local = senders - row_index * send_patch
    receive_local = receivers // send_patch * own_rows + receivers % own_rows
    live_count = edge_count[0]
    node_state = node_latent
    edge_state = edge_latent.astype(jnp.float32)
    for layer_id in range(layer_total):
        w_edge_in = edge_in[layer_id]
        w_edge_out = edge_out[layer_id]
        node_half = node_state.astype(jnp.bfloat16)
        w_edge = w_edge_in[:latent_width]
        w_send = w_edge_in[latent_width : 2 * latent_width]
        w_receive = w_edge_in[2 * latent_width :]
        send_table = lax.all_gather(
            product(node_half, w_send).astype(jnp.bfloat16), "col", axis=0, tiled=True
        ).astype(jnp.float32)
        receive_table = lax.all_gather(
            product(node_half, w_receive).astype(jnp.bfloat16), "row", axis=0, tiled=True
        ).astype(jnp.float32)

        def first_layer(
            edge_half,
            send_ids,
            receive_ids,
            send_table=send_table,
            receive_table=receive_table,
            w_edge=w_edge,
        ):
            return product(edge_half, w_edge) + send_table[send_ids] + receive_table[receive_ids]

        def edge_section(
            edge_block, send_ids, receive_ids, first_layer=first_layer, w_edge_out=w_edge_out
        ):
            first_out = first_layer(edge_block.astype(jnp.bfloat16), send_ids, receive_ids)
            hidden = jax.nn.silu(first_out).astype(jnp.bfloat16)
            return edge_block + layer_norm(product(hidden, w_edge_out))

        edge_state = edge_section(edge_state, send_local, receive_local)
        live_mask = jnp.arange(slot_total, dtype=jnp.int32) < live_count
        masked = jnp.where(live_mask[:, None], edge_state, 0.0)
        partial_value = jax.ops.segment_sum(masked, receive_local, num_segments=patch_rows)
        edge_total = lax.psum_scatter(
            partial_value.astype(jnp.bfloat16), "row", scatter_dimension=0, tiled=True
        ).astype(jnp.float32)
        node_state = node_section(node_state, edge_total, node_in[layer_id], node_out[layer_id])
    return node_state


def solution(mesh):
    placed = (
        P(("row", "col"), None),
        P(("row", "col"), None),
        P(("row", "col")),
        P(("row", "col")),
        P(("row", "col")),
        P(),
        P(),
        P(),
        P(),
    )
    return jax.shard_map(
        per_device, mesh=mesh, in_specs=placed, out_specs=P(("row", "col"), None), check_vma=False
    )
```

profile of v0, /device:TPU:0, one launch (start us, length us, event | category | flops | bytes accessed | tf_op | source)
XLA Modules:
  0.0 252.5 jit_solution(14522637842968588110)
XLA Ops:
  7.5 1.9 convolution_convert_fusion.3
  11.4 2.0 all_gather.13
  13.5 4.0 %copy.11 = bf16[2048,512]{0,1:T(8,128)(2,1)} copy(bf16[2048,512]{1,0:T(8,128)(2,1)} %param.10) | data formatting | bytes 4194304 | tf_op args[1]
  17.5 8.9 %gather_fusion.1 = f32[2048,512]{1,0:T(8,128)} fusion(f32[192,512]{1,0:T(8,128)S(1)} %convert_element_type.66, s32[2048]{0:T(1024)S(1)} %get-tuple-element.5), kind=kCustom, calls=%fused_computation.1 | custom fusion | bytes 8396800 | tf_op jit(solution)/shard_map/gather | solution.py:60
  26.5 44.2 %all-gather.3.cloned.1.call-done = bf16[1536,512]{1,0:T(8,128)(2,1)} async-done(((bf16[96,512]{1,0:T(8,128)(2,1)}), bf16[1536,512]{1,0:T(8,128)(2,1)}) %all-gather.3.cloned.1.call-update) | async-done | bytes 1572880 | tf_op jit(solution)/shard_map/all_gather | solution.py:45
  72.6 8.9 %gather_fusion = f32[2048,512]{1,0:T(8,128)} fusion(f32[1536,512]{1,0:T(8,128)S(1)} %convert_element_type.64, s32[2048]{0:T(1024)S(1)} %fusion.67), kind=kCustom, calls=%fused_computation | custom fusion | bytes 8396800 | tf_op jit(solution)/shard_map/gather | solution.py:60
  81.5 9.2 %fusion.80 = (f32[2048]{0:T(1024)S(1)}, f32[2048,512]{0,1:T(8,128)}) fusion(bf16[2,512,512]{2,1,0:T(8,128)(2,1)} %param.15, f32[2048,512]{1,0:T(8,128)} %gather_fusion.1, f32[2048,512]{1,0:T(8,128)} %gather_fusion, bf16[2048,512]{1,0:T(8,128)(2,1)} %param.10, bf16[2,1536,512]{2,1,0:T(8,128)(2,1)} %param.14), kind=kOutput, calls=%fused_computation.94 | convolution fusion | flops 2155870208 | bytes 15736832 | tf_op jit(solution)/shard_map/dot_general | solution.py:14
  90.7 2.8 %multiply_reduce_fusion.1 = f32[2048]{0:T(1024)S(1)} fusion(f32[2048,512]{0,1:T(8,128)} %get-tuple-element.8, f32[2048]{0:T(1024)S(1)} %broadcast_multiply_fusion.1), kind=kLoop, calls=%fused_computation.10 | loop fusion | flops 3143680 | bytes 4210688 | tf_op jit(solution)/shard_map/reduce_sum | solution.py:9
  94.2 2.8 %broadcast_select_fusion = f32[2048,512]{0,1:T(8,128)} fusion(pred[2048]{0:T(1024)(128)(4,1)S(1)} %iota_compare_fusion, f32[2048]{0:T(1024)S(1)} %add_rsqrt_fusion.1, f32[2048,512]{0,1:T(8,128)S(1)} %copy-done, f32[2048]{0:T(1024)S(1)} %broadcast_multiply_fusion.1, bf16[2048,512]{0,1:T(8,128)(2,1)S(1)} %copy-done.2), kind=kLoop, calls=%fused_computation.13 | loop fusion | flops 5242880 | bytes 10504192 | tf_op jit(solution)/shard_map/jit(_where)/select_n | solution.py:71
  97.0 5.5 %copy.12 = f32[2048,512]{1,0:T(8,128)} copy(f32[2048,512]{0,1:T(8,128)} %broadcast_select_fusion) | data formatting | bytes 8388608 | tf_op jit(solution)/shard_map/jit(_where)/select_n | solution.py:71
  102.5 13.4 %scatter_custom_fusion = f32[192,512]{1,0:T(8,128)S(1)} fusion(s32[2048]{0:T(1024)S(1)} %get-tuple-element.6, f32[2048,512]{1,0:T(8,128)} %copy.12, f32[]{:T(128)} %constant.45.clone.1), kind=kCustom, calls=%fused_computation.62 | custom fusion | flops 1048576 | bytes 393728 | tf_op jit(solution)/shard_map/scatter-add | solution.py:72
  116.6 6.4 %reduce-scatter.3.cloned.1.call-done = bf16[96,512]{1,0:T(8,128)(2,1)} async-done(((bf16[192,512]{1,0:T(8,128)(2,1)}), bf16[96,512]{1,0:T(8,128)(2,1)}) %reduce-scatter.3.cloned.1.call-update) | async-done | bytes 98320 | tf_op jit(solution)/shard_map/reduce_scatter | solution.py:73
  123.0 1.9 fusion.83
  125.3 1.9 convolution_convert_fusion.1
  128.6 2.1 all_gather.15
  130.8 8.9 %gather_fusion.3 = f32[2048,512]{1,0:T(8,128)} fusion(f32[192,512]{1,0:T(8,128)S(1)} %convert_element_type.75, s32[2048]{0:T(1024)S(1)} %get-tuple-element.5), kind=kCustom, calls=%fused_computation.3 | custom fusion | bytes 8396800 | tf_op jit(solution)/shard_map/gather | solution.py:60
  139.7 46.7 %all-gather.5.cloned.1.call-done = bf16[1536,512]{1,0:T(8,128)(2,1)} async-done(((bf16[96,512]{1,0:T(8,128)(2,1)}), bf16[1536,512]{1,0:T(8,128)(2,1)}) %all-gather.5.cloned.1.call-update) | async-done | bytes 1572880 | tf_op jit(solution)/shard_map/all_gather | solution.py:45
  188.3 8.9 %gather_fusion.2 = f32[2048,512]{1,0:T(8,128)} fusion(f32[1536,512]{1,0:T(8,128)S(1)} %convert_element_type.73, s32[2048]{0:T(1024)S(1)} %copy-done.10), kind=kCustom, calls=%fused_computation.2 | custom fusion | bytes 8396800 | tf_op jit(solution)/shard_map/gather | solution.py:60
  197.2 10.9 %fusion.88 = (f32[2048]{0:T(1024)S(1)}, f32[2048,512]{0,1:T(8,128)}) fusion(bf16[2,512,512]{2,1,0:T(8,128)(2,1)} %param.15, f32[2048,512]{1,0:T(8,128)} %gather_fusion.3, f32[2048,512]{1,0:T(8,128)} %gather_fusion.2, bf16[2048,512]{0,1:T(8,128)(2,1)} %copy.11, f32[2048,512]{0,1:T(8,128)} %get-tuple-element.8, f32[2048]{0:T(1024)} %copy-done.11, ...), kind=kOutput, calls=%fused_computation.96 | convolution fusion | flops 2161113088 | bytes 19947520 | tf_op jit(solution)/shard_map/dot_general | solution.py:14
  208.1 2.8 %multiply_reduce_fusion = f32[2048]{0:T(1024)S(1)} fusion(f32[2048,512]{0,1:T(8,128)} %get-tuple-element.12, f32[2048]{0:T(1024)S(1)} %broadcast_multiply_fusion), kind=kLoop, calls=%fused_computation.7 | loop fusion | flops 3143680 | bytes 4210688 | tf_op jit(solution)/shard_map/reduce_sum | solution.py:9
  211.5 5.7 %add_select_fusion = f32[2048,512]{0,1:T(8,128)} fusion(f32[2048,512]{0,1:T(8,128)} %get-tuple-element.12, f32[2048]{0:T(1024)S(1)} %add_rsqrt_fusion, f32[2048]{0:T(1024)S(1)} %broadcast_multiply_fusion, pred[2048]{0:T(1024)(128)(4,1)S(1)} %copy-done.14, f32[2048]{0:T(1024)S(1)} %copy-done.12, f32[2048,512]{0,1:T(8,128)S(1)} %copy-done.1, ...), kind=kLoop, calls=%fused_computation.6 | loop fusion | flops 8388608 | bytes 14714880 | tf_op jit(solution)/shard_map/jit(_where)/select_n | solution.py:71
  217.2 5.5 %copy.13 = f32[2048,512]{1,0:T(8,128)} copy(f32[2048,512]{0,1:T(8,128)} %add_select_fusion) | data formatting | bytes 8388608 | tf_op jit(solution)/shard_map/jit(_where)/select_n | solution.py:71
  222.7 13.3 %scatter_custom_fusion.1 = f32[192,512]{1,0:T(8,128)S(1)} fusion(s32[2048]{0:T(1024)} %copy-done.16, f32[2048,512]{1,0:T(8,128)} %copy.13, f32[]{:T(128)} %constant.45.clone.1), kind=kCustom, calls=%fused_computation.60 | custom fusion | flops 1048576 | bytes 393728 | tf_op jit(solution)/shard_map/scatter-add | solution.py:72
  236.8 6.5 %reduce-scatter.5.cloned.1.call-done = bf16[96,512]{1,0:T(8,128)(2,1)} async-done(((bf16[192,512]{1,0:T(8,128)(2,1)}), bf16[96,512]{1,0:T(8,128)(2,1)}) %reduce-scatter.5.cloned.1.call-update) | async-done | bytes 98320 | tf_op jit(solution)/shard_map/reduce_scatter | solution.py:73
  (81 shorter events, 13.2 us)
Async XLA Ops:
  6.5 11.0 %copy-start.15 = (s32[2048]{0:T(1024)S(1)}, s32[2048]{0:T(1024)}, u32[]{:S(2)}) copy-start(s32[2048]{0:T(1024)} %param.12) | copy-start | bytes 24580
  6.5 64.2 %all-gather.3.cloned.1.call-start = ((), (), s32[]{:S(2)}) async-start(), calls=%async_computation.2 | async-start | bytes 1671168 | tf_op jit(solution)/shard_map/all_gather | solution.py:45
  7.5 3.9 %copy-start.5 = (bf16[96,512]{1,0:T(8,128)(2,1)}, bf16[96,512]{1,0:T(8,128)(2,1)S(1)}, u32[]{:S(2)}) copy-start(bf16[96,512]{1,0:T(8,128)(2,1)S(1)} %convert_element_type.61) | copy-start | bytes 294916
  9.5 113.6 %reduce-scatter.3.cloned.1.call-start = ((), (), s32[]{:S(2)}) async-start(), calls=%async_computation.3 | async-start | bytes 294912 | tf_op jit(solution)/shard_map/reduce_scatter | solution.py:73
  17.5 84.9 %copy-start.16 = (s32[2048]{0:T(1024)}, s32[2048]{0:T(1024)S(1)}, u32[]{:S(2)}) copy-start(s32[2048]{0:T(1024)S(1)} %get-tuple-element.6) | copy-start | bytes 24580
  17.5 9.0 %copy-start.17 = (s32[2048]{0:T(1024)S(1)}, s32[2048]{0:T(1024)}, u32[]{:S(2)}) copy-start(s32[2048]{0:T(1024)} %param.11) | copy-start | bytes 24580
  26.5 67.0 %copy-start.13 = (pred[2048]{0:T(1024)(128)(4,1)}, pred[2048]{0:T(1024)(128)(4,1)S(1)}, u32[]{:S(2)}) copy-start(pred[2048]{0:T(1024)(128)(4,1)S(1)} %iota_compare_fusion) | copy-start | bytes 6148
  26.5 55.0 %copy-start.9 = (s32[2048]{0:T(1024)}, s32[2048]{0:T(1024)S(1)}, u32[]{:S(2)}) copy-start(s32[2048]{0:T(1024)S(1)} %fusion.67) | copy-start | bytes 24580
  81.5 12.0 %copy-start.2 = (bf16[2048,512]{0,1:T(8,128)(2,1)S(1)}, bf16[2048,512]{0,1:T(8,128)(2,1)}, u32[]{:S(2)}) copy-start(bf16[2048,512]{0,1:T(8,128)(2,1)} %copy.11) | copy-start | bytes 6291460
  90.7 3.4 %copy-start = (f32[2048,512]{0,1:T(8,128)S(1)}, f32[2048,512]{0,1:T(8,128)}, u32[]{:S(2)}) copy-start(f32[2048,512]{0,1:T(8,128)} %get-tuple-element.8) | copy-start | bytes 12582916
  97.0 26.1 %copy-start.6 = (bf16[96,512]{1,0:T(8,128)(2,1)S(1)}, bf16[96,512]{1,0:T(8,128)(2,1)}, u32[]{:S(2)}) copy-start(bf16[96,512]{1,0:T(8,128)(2,1)} %copy-done.5) | copy-start | bytes 294916
  97.0 26.1 %copy-start.23 = (bf16[2,512,512]{2,1,0:T(8,128)(2,1)S(1)}, bf16[2,512,512]{2,1,0:T(8,128)(2,1)}, u32[]{:S(2)}) copy-start(bf16[2,512,512]{2,1,0:T(8,128)(2,1)} %param.17) | copy-start | bytes 3145732
  102.5 22.7 %copy-start.4 = (f32[96,512]{1,0:T(8,128)S(1)}, f32[96,512]{1,0:T(8,128)}, u32[]{:S(2)}) copy-start(f32[96,512]{1,0:T(8,128)} %param.9) | copy-start | bytes 589828
  116.6 69.9 %all-gather.5.cloned.1.call-start = ((), (), s32[]{:S(2)}) async-start(), calls=%async_computation.4 | async-start | bytes 1671168 | tf_op jit(solution)/shard_map/all_gather | solution.py:45
  124.9 3.6 %copy-start.18 = (f32[96]{0:T(128)}, f32[96]{0:T(128)S(1)}, u32[]{:S(2)}) copy-start(f32[96]{0:T(128)S(1)} %broadcast_multiply_fusion.3) | copy-start | bytes 1156
  127.3 116.0 %reduce-scatter.5.cloned.1.call-start = ((), (), s32[]{:S(2)}) async-start(), calls=%async_computation.5 | async-start | bytes 294912 | tf_op jit(solution)/shard_map/reduce_scatter | solution.py:73
  139.7 48.6 %copy-start.10 = (s32[2048]{0:T(1024)S(1)}, s32[2048]{0:T(1024)}, u32[]{:S(2)}) copy-start(s32[2048]{0:T(1024)} %copy-done.9) | copy-start | bytes 24580
  197.2 13.7 %copy-start.3 = (bf16[2048,512]{0,1:T(8,128)(2,1)S(1)}, bf16[2048,512]{0,1:T(8,128)(2,1)}, u32[]{:S(2)}) copy-start(bf16[2048,512]{0,1:T(8,128)(2,1)} %copy.11) | copy-start | bytes 6291460
  208.1 3.4 %copy-start.12 = (f32[2048]{0:T(1024)S(1)}, f32[2048]{0:T(1024)}, u32[]{:S(2)}) copy-start(f32[2048]{0:T(1024)} %copy-done.11) | copy-start | bytes 24580
  208.1 3.5 %copy-start.14 = (pred[2048]{0:T(1024)(128)(4,1)S(1)}, pred[2048]{0:T(1024)(128)(4,1)}, u32[]{:S(2)}) copy-start(pred[2048]{0:T(1024)(128)(4,1)} %copy-done.13) | copy-start | bytes 6148
  217.2 26.1 %copy-start.8 = (bf16[96,512]{1,0:T(8,128)(2,1)S(1)}, bf16[96,512]{1,0:T(8,128)(2,1)}, u32[]{:S(2)}) copy-start(bf16[96,512]{1,0:T(8,128)(2,1)} %copy-done.7) | copy-start | bytes 294916
  217.2 26.1 %copy-start.22 = (bf16[2,1024,512]{2,1,0:T(8,128)(2,1)S(1)}, bf16[2,1024,512]{2,1,0:T(8,128)(2,1)}, u32[]{:S(2)}) copy-start(bf16[2,1024,512]{2,1,0:T(8,128)(2,1)} %param.16) | copy-start | bytes 6291460
  222.7 22.5 %copy-start.19 = (f32[96]{0:T(128)S(1)}, f32[96]{0:T(128)}, u32[]{:S(2)}) copy-start(f32[96]{0:T(128)} %copy-done.18) | copy-start | bytes 1156
  222.7 22.5 %copy-start.21 = (f32[96]{0:T(128)S(1)}, f32[96]{0:T(128)}, u32[]{:S(2)}) copy-start(f32[96]{0:T(128)} %copy-done.20) | copy-start | bytes 1156
  (4 other events, 13.0 us)
Sparse Core Ops, SparseCore 0:
  10.1 60.5 all-gather.2
  116.7 6.2 reduce-scatter.2
  127.4 59.0 all-gather.4
  236.9 6.2 reduce-scatter.4
where the time goes:
time: 253 us
  waiting for transfers between devices  104 us (41%)
  local copies, waits for them, and re-layouts  51.9 us (21%)
  other arithmetic  48.2 us (19%)
  matrix products  30.1 us (12%)
  between operations  14.1 us (6%)
  blocking collectives  4.18 us (2%)
    all_gather x2, waiting for transfers between devices, per_device(): lax.all_gather(product(node_half, w_send).astype(jnp.bfloat16), 'col', ax...  90.9 us
    dot_general x8, matrix products, product(): return jnp.dot(matrix, weight, preferred_element_type=jnp.float32)  30.1 us
    scatter-add x2, other arithmetic, per_device(): jax.ops.segment_sum(masked, receive_local, num_segments=patch_rows)  26.7 us
    gather x2, local copies, waits for them, and re-layouts, first_layer(): receive_table[receive_ids]  17.9 us
    gather x2, local copies, waits for them, and re-layouts, first_layer(): send_table[send_ids]  17.8 us
    reduce_scatter x2, waiting for transfers between devices, per_device(): lax.psum_scatter(partial_value.astype(jnp.bfloat16), 'row', scatter_dimen...  12.9 us
    select_n x2, local copies, waits for them, and re-layouts, per_device(): masked = jnp.where(live_mask[:, None], edge_state, 0.0)  11 us
    select_n x2, other arithmetic, per_device(): masked = jnp.where(live_mask[:, None], edge_state, 0.0)  8.5 us
  transfers between devices with their start and end apart: 4, of which 4 were waited for; matrix products, arithmetic and copies ran while one was open for 10% of the time, Pallas kernels for 0%

commit v1 on v0

v1 whole, which is shorter than its diff:
```python
import functools

import jax
import jax.numpy as jnp
from jax import lax
from jax.experimental import pallas as pl
from jax.experimental.pallas import tpu as pltpu
from jax.sharding import PartitionSpec as P

MESH = pl.DeviceIdType.MESH
HALVES = 2
EDGE_ROWS = 256


def layer_norm(values):
    centre = values - jnp.mean(values, axis=-1, keepdims=True)
    spread = jnp.mean(centre * centre, axis=-1, keepdims=True)
    return centre * lax.rsqrt(spread + 1e-05)


def product(matrix, weight):
    return jnp.dot(matrix, weight, preferred_element_type=jnp.float32)


def silu(values):
    half = 0.5 * values
    return half + half * jnp.tanh(half)


def kernel(
    lines,
    ids_ref,
    receive_row_ref,
    node_hbm,
    edge_hbm,
    edge_in_hbm,
    edge_out_hbm,
    node_in_hbm,
    node_out_hbm,
    out_ref,
    node_state,
    edge_half,
    edge_state,
    acc,
    onehot,
    scatter_hot,
    table,
    w_edge_in,
    w_edge_out,
    w_node_in,
    w_node_out,
    partial_sum,
    part_out,
    part_in,
    node_first,
    load_sem,
    gather_send,
    gather_recv,
    row_send,
    row_recv,
    part_send,
    part_recv,
):
    layers, _, width = w_edge_in.shape
    own = node_state.shape[0]
    slots = edge_half.shape[0]
    rows = part_in.shape[1] + 1
    piece = own // HALVES
    group = HALVES * lines * piece
    send_rows = 4 * group
    recv_rows = rows * own
    tiles = slots // EDGE_ROWS

    row_me = lax.axis_index("row")
    col_me = lax.axis_index("col")
    a_me = col_me // 4
    inner = lax.rem(col_me, 4)
    b_me = inner // 2
    c_me = lax.rem(inner, 2)
    flip_b = a_me * 4 + (1 - b_me) * 2 + c_me
    flip_c = a_me * 4 + b_me * 2 + (1 - c_me)

    def line_peer(step):
        return lax.rem(a_me + lines - step, lines) * 4 + inner

    def row_peer(step):
        return lax.rem(row_me + rows + step, rows)

    barrier = pltpu.get_barrier_semaphore()
    for step in range(1, lines):
        pl.semaphore_signal(barrier, inc=1, device_id={"col": line_peer(step)}, device_id_type=MESH)
    for target in (flip_b, flip_c):
        pl.semaphore_signal(barrier, inc=1, device_id={"col": target}, device_id_type=MESH)
    for step in range(1, rows):
        pl.semaphore_signal(barrier, inc=1, device_id={"row": row_peer(step)}, device_id_type=MESH)

    loads = {}

    def load(name, source, target):
        copy = pltpu.make_async_copy(source, target, load_sem.at[len(loads)])
        copy.start()
        loads[name] = copy

    load("node", node_hbm, node_state)
    for layer_id in range(layers):
        for name, part in (("send", 1), ("receive", 2), ("edge", 0)):
            span = pl.ds(part * width, width)
            load(
                (name, layer_id),
                edge_in_hbm.at[layer_id, span],
                w_edge_in.at[layer_id, span],
            )
            if layer_id == 0 and name == "receive":
                load("edges", edge_hbm, edge_half)
        load(("node_in", layer_id), node_in_hbm.at[layer_id], w_node_in.at[layer_id])
        load(("edge_out", layer_id), edge_out_hbm.at[layer_id], w_edge_out.at[layer_id])
        load(("node_out", layer_id), node_out_hbm.at[layer_id], w_node_out.at[layer_id])

    def slot_row(half, slot):
        kind, line = slot // lines, slot % lines
        return kind * group + half * lines * piece + line * piece

    pending = []
    loads["node"].wait()
    for layer_id in range(layers):
        copies = {}

        def push(half, source, slot, target, layer_id=layer_id, copies=copies):
            copy = pltpu.make_async_remote_copy(
                src_ref=table.at[layer_id, pl.ds(slot_row(half, source), piece)],
                dst_ref=table.at[layer_id, pl.ds(slot_row(half, slot), piece)],
                send_sem=gather_send.at[layer_id, half, slot],
                recv_sem=gather_recv.at[layer_id, half, slot],
                device_id={"col": target},
                device_id_type=MESH,
            )
            copy.start()
            copies[half, slot] = copy
            pending.append(copy)

        first_target = (flip_c, flip_b)
        second_target = (flip_b, flip_c)
        w_edge = w_edge_in.at[layer_id]
        node_half = node_state[...].astype(jnp.bfloat16)

        loads["send", layer_id].wait()
        sent = product(node_half, w_edge[width : 2 * width, :]).astype(jnp.bfloat16)
        for half in range(HALVES):
            table[layer_id, pl.ds(slot_row(half, 0), piece), :] = sent[
                half * piece : (half + 1) * piece
            ]
        if layer_id == 0:
            pl.semaphore_wait(barrier, lines - 1 + 2 + rows - 1)
        for half in range(HALVES):
            push(half, 0, lines, first_target[half])
        for step in range(1, lines):
            for half in range(HALVES):
                push(half, 0, step, line_peer(step))
        for half in range(HALVES):
            push(half, 0, 2 * lines, second_target[half])

        loads["receive", layer_id].wait()
        table[layer_id, pl.ds(send_rows, own), :] = product(
            node_half, w_edge[2 * width : 3 * width, :]
        ).astype(jnp.bfloat16)
        row_copies = []
        for step in range(1, rows):
            copy = pltpu.make_async_remote_copy(
                src_ref=table.at[layer_id, pl.ds(send_rows, own)],
                dst_ref=table.at[layer_id, pl.ds(send_rows + step * own, own)],
                send_sem=row_send.at[layer_id, step - 1],
                recv_sem=row_recv.at[layer_id, step - 1],
                device_id={"row": row_peer(-step)},
                device_id_type=MESH,
            )
            copy.start()
            row_copies.append(copy)
            pending.append(copy)

        loads["node_in", layer_id].wait()
        node_first[...] = product(node_half, w_node_in[layer_id, :width, :])

        loads["edge", layer_id].wait()
        if layer_id == 0:
            loads["edges"].wait()

        def early(tile, carry, layer_id=layer_id, w_edge=w_edge):
            span = pl.ds(pl.multiple_of(tile * EDGE_ROWS, EDGE_ROWS), EDGE_ROWS)
            acc[span, :] = product(edge_half[span, :], w_edge[:width, :])
            if layer_id == 0:
                ids = ids_ref[span, :]
                send_lane = lax.broadcasted_iota(jnp.int32, (EDGE_ROWS, send_rows), 1)
                onehot[span, :send_rows] = jnp.where(send_lane == ids[:, 0:1], 1.0, 0.0).astype(
                    jnp.bfloat16
                )
                recv_lane = lax.broadcasted_iota(jnp.int32, (EDGE_ROWS, recv_rows), 1)
                onehot[span, send_rows:] = jnp.where(recv_lane == ids[:, 1:2], 1.0, 0.0).astype(
                    jnp.bfloat16
                )
            return carry

        def forward_line(step):
            for half in range(HALVES):
                copies[half, step].wait_recv()
                push(half, step, lines + step, first_target[half])
                push(half, step, 2 * lines + step, second_target[half])

        def forward_first(step):
            for half in range(HALVES):
                copies[half, lines + step].wait_recv()
                push(half, lines + step, 3 * lines + step, second_target[half])

        middle_tile = tiles // 2
        lax.fori_loop(0, middle_tile, early, 0)
        forward_first(0)
        forward_line(1)
        lax.fori_loop(middle_tile, tiles, early, 0)
        if layer_id == 0:
            slot_id = lax.broadcasted_iota(jnp.int32, (recv_rows, slots), 0)
            scatter_hot[...] = jnp.where(slot_id == receive_row_ref[...], 1.0, 0.0).astype(
                jnp.bfloat16
            )
        for step in range(2, lines):
            forward_line(step)
        for step in range(1, lines):
            forward_first(step)
        for copy in row_copies:
            copy.wait_recv()

        def middle(tile, carry, layer_id=layer_id):
            span = pl.ds(pl.multiple_of(tile * EDGE_ROWS, EDGE_ROWS), EDGE_ROWS)
            acc[span, :] += product(
                onehot[span, : 2 * group], table[layer_id, : 2 * group, :]
            ) + product(onehot[span, send_rows:], table[layer_id, send_rows:, :])
            return carry

        lax.fori_loop(0, tiles, middle, 0)
        for step in range(2 * lines):
            for half in range(HALVES):
                copies[half, 2 * lines + step].wait_recv()

        loads["edge_out", layer_id].wait()
        partial_sum[...] = jnp.zeros_like(partial_sum)

        def late(tile, carry, layer_id=layer_id):
            span = pl.ds(pl.multiple_of(tile * EDGE_ROWS, EDGE_ROWS), EDGE_ROWS)
            first_out = acc[span, :] + product(
                onehot[span, 2 * group : send_rows], table[layer_id, 2 * group : send_rows, :]
            )
            hidden = silu(first_out).astype(jnp.bfloat16)
            if layer_id == 0:
                before = edge_half[span, :].astype(jnp.float32)
            else:
                before = edge_state[span, :]
            after = before + layer_norm(product(hidden, w_edge_out[layer_id]))
            after_half = after.astype(jnp.bfloat16)
            if layer_id < layers - 1:
                edge_state[span, :] = after
                edge_half[span, :] = after_half
            partial_sum[...] += product(scatter_hot[:, span], after_half)
            return carry

        lax.fori_loop(0, tiles, late, 0)

        part_copies = []
        for step in range(1, rows):
            part_out[layer_id, step - 1] = partial_sum[
                step * own : (step + 1) * own, :
            ].astype(jnp.bfloat16)
            copy = pltpu.make_async_remote_copy(
                src_ref=part_out.at[layer_id, step - 1],
                dst_ref=part_in.at[layer_id, step - 1],
                send_sem=part_send.at[layer_id, step - 1],
                recv_sem=part_recv.at[layer_id, step - 1],
                device_id={"row": row_peer(step)},
                device_id_type=MESH,
            )
            copy.start()
            part_copies.append(copy)
            pending.append(copy)
        edge_total = partial_sum[:own, :]
        for step, copy in enumerate(part_copies):
            copy.wait_recv()
            edge_total = edge_total + part_in[layer_id, step].astype(jnp.float32)

        loads["node_out", layer_id].wait()
        first_out = node_first[...] + product(
            edge_total.astype(jnp.bfloat16), w_node_in[layer_id, width:, :]
        )
        hidden = silu(first_out).astype(jnp.bfloat16)
        after = node_state[...] + layer_norm(product(hidden, w_node_out[layer_id]))
        if layer_id < layers - 1:
            node_state[...] = after
        else:
            out_ref[...] = after
    for copy in pending:
        copy.wait_send()


def per_device(
    node_latent, edge_latent, senders, receivers, edge_count, edge_in, edge_out, node_in, node_out
):
    own, width = node_latent.shape
    slots = edge_latent.shape[0]
    layers = edge_in.shape[0]
    cols = lax.axis_size("col")
    rows = lax.axis_size("row")
    lines = cols // 4
    piece = own // HALVES
    row_me = lax.axis_index("row")
    col_me = lax.axis_index("col")
    send_patch = own * cols
    local = senders - row_me * send_patch
    block, offset = local // own, local % own
    line = (block // 4 - col_me // 4) % lines
    flip_b = (block // 2 % 2) ^ (col_me // 2 % 2)
    flip_c = (block % 2) ^ (col_me % 2)
    half = offset // piece
    first = jnp.where(half == 0, flip_c, flip_b)
    second = jnp.where(half == 0, flip_b, flip_c)
    send_slot = (
        (second * 2 + first) * (HALVES * lines * piece)
        + half * (lines * piece)
        + line * piece
        + offset % piece
    )
    receive_slot = (receivers // send_patch - row_me) % rows * own + receivers % own
    ids = jnp.stack([send_slot, receive_slot], axis=1)
    live_mask = jnp.arange(slots, dtype=jnp.int32) < edge_count[0]
    receive_row = jnp.where(live_mask, receive_slot, -1)[None, :]

    send_rows, recv_rows = cols * own, rows * own
    half_type, full_type = jnp.bfloat16, jnp.float32
    vmem = pl.BlockSpec(memory_space=pltpu.VMEM)
    anywhere = pl.BlockSpec(memory_space=pl.ANY)
    dma = pltpu.SemaphoreType.DMA
    return pl.pallas_call(
        functools.partial(kernel, lines),
        out_shape=jax.ShapeDtypeStruct((own, width), full_type),
        in_specs=[vmem] * 2 + [anywhere] * 6,
        out_specs=vmem,
        scratch_shapes=[
            pltpu.VMEM((own, width), full_type),
            pltpu.VMEM((slots, width), half_type),
            pltpu.VMEM((slots, width), full_type),
            pltpu.VMEM((slots, width), full_type),
            pltpu.VMEM((slots, send_rows + recv_rows), half_type),
            pltpu.VMEM((recv_rows, slots), half_type),
            pltpu.VMEM((layers, send_rows + recv_rows, width), half_type),
            pltpu.VMEM(edge_in.shape, half_type),
            pltpu.VMEM(edge_out.shape, half_type),
            pltpu.VMEM(node_in.shape, half_type),
            pltpu.VMEM(node_out.shape, half_type),
            pltpu.VMEM((recv_rows, width), full_type),
            pltpu.VMEM((layers, rows - 1, own, width), half_type),
            pltpu.VMEM((layers, rows - 1, own, width), half_type),
            pltpu.VMEM((own, width), full_type),
            dma((2 + 6 * layers,)),
            dma((layers, HALVES, cols)),
            dma((layers, HALVES, cols)),
            dma((layers, rows - 1)),
            dma((layers, rows - 1)),
            dma((layers, rows - 1)),
            dma((layers, rows - 1)),
        ],
        compiler_params=pltpu.CompilerParams(
            collective_id=0, has_side_effects=True, vmem_limit_bytes=60 * 1024 * 1024
        ),
    )(ids, receive_row, node_latent, edge_latent, edge_in, edge_out, node_in, node_out)


def solution(mesh):
    placed = (
        P(("row", "col"), None),
        P(("row", "col"), None),
        P(("row", "col")),
        P(("row", "col")),
        P(("row", "col")),
        P(),
        P(),
        P(),
        P(),
    )
    return jax.shard_map(
        per_device, mesh=mesh, in_specs=placed, out_specs=P(("row", "col"), None), check_vma=False
    )
```

time: 253 us -> 70.2 us (0.28)
  waiting for transfers between devices: 104 us -> 0 us
  Pallas kernels: 0 us -> 64.2 us
  local copies, waits for them, and re-layouts: 51.9 us -> 2.98 us
  other arithmetic: 48.2 us -> 2.08 us
  matrix products: 30.1 us -> 0 us
  between operations: 14.1 us -> 0.67 us
  blocking collectives: 4.18 us -> 0 us
    all_gather x2 -> x0, waiting for transfers between devices: 90.9 us -> none  [per_device(): lax.all_gather(product(node_half, w_send).astype(jnp.bfloat16), 'col', ax...]
    pallas_call x0 -> x1, Pallas kernels: none -> 64.2 us  [per_device(): pl.pallas_call(functools.partial(kernel, lines), out_shape=jax.ShapeDtype...]
    gather x4 -> x0, local copies, waits for them, and re-layouts: 35.7 us -> none  [the longest x2 17.9 us: first_layer(): receive_table[receive_ids]]
    dot_general x8 -> x0, matrix products: 30.1 us -> none  [product(): return jnp.dot(matrix, weight, preferred_element_type=jnp.float32)]
    scatter-add x2 -> x0, other arithmetic: 26.7 us -> none  [per_device(): jax.ops.segment_sum(masked, receive_local, num_segments=patch_rows)]
    reduce_scatter x2 -> x0, waiting for transfers between devices: 12.9 us -> none  [per_device(): lax.psum_scatter(partial_value.astype(jnp.bfloat16), 'row', scatter_dimen...]
    select_n x2 -> x0, local copies, waits for them, and re-layouts: 11 us -> none  [per_device(): masked = jnp.where(live_mask[:, None], edge_state, 0.0)]
    select_n x2 -> x1, other arithmetic: 8.5 us -> 1.32 us  [per_device(): receive_row = jnp.where(live_mask, receive_slot, -1)[None, :]]
  transfers between devices with their start and end apart: 4 -> 0, of which waited for: 4 -> 0; matrix products, arithmetic and copies ran while one was open for 10% -> 0% of each run, Pallas kernels for 0% -> 0%
where the time goes in v1:
time: 70.2 us; the launch traced here: 69.9 us
  Pallas kernels  64.2 us (91%)
  local copies, waits for them, and re-layouts  2.98 us (4%)
  other arithmetic  2.08 us (3%)
    pallas_call x1, Pallas kernels, per_device(): pl.pallas_call(functools.partial(kernel, lines), out_shape=jax.ShapeDtype...  64.2 us
    unnamed x1, local copies, waits for them, and re-layouts  1.62 us

profile of v1, /device:TPU:0, one launch (start us, length us, event | category | flops | bytes accessed | tf_op | source)
XLA Modules:
  0.0 69.9 jit_solution(16762551635627204310)
XLA Ops:
  0.7 0.7 %fusion.8 = s32[2048]{0:T(1024)S(1)} fusion(s32[2048]{0:T(1024)} %param.11, s32[]{:T(128)S(6)} %select_n.87, s32[]{:T(128)S(6)} %select_n.83, s32[]{:T(128)S(6)} %select_n.81, s32[]{:T(128)S(6)} %mul.27), kind=kLoop, calls=%fused_computation.32 | loop fusion | flops 184320 | bytes 16400 | tf_op jit(solution)/shard_map/add | solution.py:322
  1.4 1.3 %fusion.16 = (s32[2048]{0:T(1024)}, s32[2048]{0:T(1024)S(1)}) fusion(s32[]{:T(128)} %bitcast.4, s32[2048]{0:T(1024)} %param.12, s32[]{:T(128)S(6)} %axis_index.23), kind=kLoop, calls=%fused_computation.46 | loop fusion | flops 61440 | bytes 24584 | tf_op jit(solution)/shard_map/jit(_where)/select_n | solution.py:330
  2.7 1.4 %copy.12.ids_ref = s32[2048,2]{1,0:T(8,128)} copy(s32[2048,2]{0,1:T(2,128)S(1)} %pad_add_fusion) | data formatting | bytes 32768 | tf_op jit(solution)/shard_map/stack | solution.py:328
  4.1 64.2 %shard_map.91 = f32[96,512]{1,0:T(8,128)} custom-call(s32[2048,2]{1,0:T(8,128)} %copy.12.ids_ref, s32[1,2048]{1,0:T(1,128)} %bitcast.5, f32[96,512]{1,0:T(8,128)} %node_hbm.1, bf16[2048,512]{1,0:T(8,128)(2,1)} %edge_hbm.1, bf16[2,1536,512]{2,1,0:T(8,128)(2,1)} %edge_in_hbm.1, bf16[2,512,512]{2,1,0:T(8,128)(2,1)} %edge_out_hbm.1, ...), custom_call_target="tpu_custom_call" | custom-call | tf_op jit(solution)/shard_map/pallas_call | solution.py:337
  68.3 1.6 %copy.15 = f32[96,512]{1,0:T(8,128)} copy(f32[96,512]{1,0:T(8,128)} %shard_map.91) | data formatting | bytes 393216
  (1 shorter events, 0.0 us)

commit v2 on v1

--- a/solution.py
+++ b/solution.py
@@ -9,7 +9,8 @@
 
 MESH = pl.DeviceIdType.MESH
 HALVES = 2
-EDGE_ROWS = 256
+EDGE_ROWS = 1024
+CHUNK = 128
 
 
 def layer_norm(values):
@@ -29,8 +30,9 @@
 
 def kernel(
     lines,
-    ids_ref,
-    receive_row_ref,
+    count_ref,
+    senders_ref,
+    receivers_ref,
     node_hbm,
     edge_hbm,
     edge_in_hbm,
@@ -53,6 +55,7 @@
     part_out,
     part_in,
     node_first,
+    places,
     load_sem,
     gather_send,
     gather_recv,
@@ -101,20 +104,57 @@
         copy.start()
         loads[name] = copy
 
+    def load_edge_in(layer_id, name, part):
+        span = pl.ds(part * width, width)
+        load((name, layer_id), edge_in_hbm.at[layer_id, span], w_edge_in.at[layer_id, span])
+
+    def load_rest():
+        for layer_id in range(layers):
+            if layer_id > 0:
+                load_edge_in(layer_id, "send", 1)
+            load_edge_in(layer_id, "receive", 2)
+            load(("node_in", layer_id), node_in_hbm.at[layer_id], w_node_in.at[layer_id])
+            load_edge_in(layer_id, "edge", 0)
+            if layer_id == 0:
+                load("edges", edge_hbm, edge_half)
+            load(("edge_out", layer_id), edge_out_hbm.at[layer_id], w_edge_out.at[layer_id])
+            load(("node_out", layer_id), node_out_hbm.at[layer_id], w_node_out.at[layer_id])
+
     load("node", node_hbm, node_state)
-    for layer_id in range(layers):
-        for name, part in (("send", 1), ("receive", 2), ("edge", 0)):
-            span = pl.ds(part * width, width)
-            load(
-                (name, layer_id),
-                edge_in_hbm.at[layer_id, span],
-                w_edge_in.at[layer_id, span],
-            )
-            if layer_id == 0 and name == "receive":
-                load("edges", edge_hbm, edge_half)
-        load(("node_in", layer_id), node_in_hbm.at[layer_id], w_node_in.at[layer_id])
-        load(("edge_out", layer_id), edge_out_hbm.at[layer_id], w_edge_out.at[layer_id])
-        load(("node_out", layer_id), node_out_hbm.at[layer_id], w_node_out.at[layer_id])
+    load_edge_in(0, "send", 1)
+
+    def floor_part(values, size):
+        return jnp.floor((values + 0.5) * (1.0 / size))
+
+    def place_edges():
+        local = (senders_ref[...] - row_me * (own * 4 * lines)).astype(jnp.float32)
+        block = floor_part(local, own)
+        offset = local - block * own
+        line = floor_part(block, 4)
+        corner = block - line * 4
+        corner_b = floor_part(corner, 2)
+        line = line - a_me.astype(jnp.float32)
+        line = jnp.where(line < 0.0, line + lines, line)
+        flipped_b = jnp.abs(corner_b - b_me.astype(jnp.float32))
+        flipped_c = jnp.abs(corner - corner_b * 2 - c_me.astype(jnp.float32))
+        half = floor_part(offset, piece)
+        first = jnp.where(half == 0.0, flipped_c, flipped_b)
+        second = jnp.where(half == 0.0, flipped_b, flipped_c)
+        places[0:1, :] = (
+            (second * 2 + first) * group
+            + half * (lines * piece)
+            + line * piece
+            + (offset - half * piece)
+        )
+        receiver = receivers_ref[...].astype(jnp.float32)
+        patch = floor_part(receiver, own * 4 * lines)
+        inside = receiver - patch * (own * 4 * lines)
+        inside = inside - floor_part(inside, own) * own
+        patch = patch - row_me.astype(jnp.float32)
+        patch = jnp.where(patch < 0.0, patch + rows, patch)
+        places[1:2, :] = patch * own + inside
+
+    place_edges()
 
     def slot_row(half, slot):
         kind, line = slot // lines, slot % lines
@@ -158,6 +198,8 @@
                 push(half, 0, step, line_peer(step))
         for half in range(HALVES):
             push(half, 0, 2 * lines, second_target[half])
+        if layer_id == 0:
+            load_rest()
 
         loads["receive", layer_id].wait()
         table[layer_id, pl.ds(send_rows, own), :] = product(
@@ -188,15 +230,26 @@
             span = pl.ds(pl.multiple_of(tile * EDGE_ROWS, EDGE_ROWS), EDGE_ROWS)
             acc[span, :] = product(edge_half[span, :], w_edge[:width, :])
             if layer_id == 0:
-                ids = ids_ref[span, :]
-                send_lane = lax.broadcasted_iota(jnp.int32, (EDGE_ROWS, send_rows), 1)
-                onehot[span, :send_rows] = jnp.where(send_lane == ids[:, 0:1], 1.0, 0.0).astype(
-                    jnp.bfloat16
-                )
-                recv_lane = lax.broadcasted_iota(jnp.int32, (EDGE_ROWS, recv_rows), 1)
-                onehot[span, send_rows:] = jnp.where(recv_lane == ids[:, 1:2], 1.0, 0.0).astype(
-                    jnp.bfloat16
-                )
+                diagonal = lax.broadcasted_iota(
+                    jnp.int32, (CHUNK, CHUNK), 0
+                ) == lax.broadcasted_iota(jnp.int32, (CHUNK, CHUNK), 1)
+                for chunk in range(EDGE_ROWS // CHUNK):
+                    part = pl.ds(
+                        pl.multiple_of(tile * EDGE_ROWS + chunk * CHUNK, CHUNK), CHUNK
+                    )
+                    for place, low, high in (
+                        (0, 0, send_rows),
+                        (1, send_rows, send_rows + recv_rows),
+                    ):
+                        column = jnp.sum(
+                            jnp.where(diagonal, places[place : place + 1, part], 0.0),
+                            axis=1,
+                            keepdims=True,
+                        ).astype(jnp.int32)
+                        lane = lax.broadcasted_iota(jnp.int32, (CHUNK, high - low), 1)
+                        onehot[part, low:high] = jnp.where(lane == column, 1.0, 0.0).astype(
+                            jnp.bfloat16
+                        )
             return carry
 
         def forward_line(step):
@@ -217,7 +270,9 @@
         lax.fori_loop(middle_tile, tiles, early, 0)
         if layer_id == 0:
             slot_id = lax.broadcasted_iota(jnp.int32, (recv_rows, slots), 0)
-            scatter_hot[...] = jnp.where(slot_id == receive_row_ref[...], 1.0, 0.0).astype(
+            live = lax.broadcasted_iota(jnp.int32, (1, slots), 1) < count_ref[0]
+            target = jnp.where(live, places[1:2, :], -1.0).astype(jnp.int32)
+            scatter_hot[...] = jnp.where(slot_id == target, 1.0, 0.0).astype(
                 jnp.bfloat16
             )
         for step in range(2, lines):
@@ -234,10 +289,22 @@
             ) + product(onehot[span, send_rows:], table[layer_id, send_rows:, :])
             return carry
 
+        def third(tile, carry, layer_id=layer_id):
+            span = pl.ds(pl.multiple_of(tile * EDGE_ROWS, EDGE_ROWS), EDGE_ROWS)
+            acc[span, :] += product(
+                onehot[span, 2 * group : 3 * group],
+                table[layer_id, 2 * group : 3 * group, :],
+            )
+            return carry
+
         lax.fori_loop(0, tiles, middle, 0)
-        for step in range(2 * lines):
+        for step in range(lines):
             for half in range(HALVES):
                 copies[half, 2 * lines + step].wait_recv()
+        lax.fori_loop(0, tiles, third, 0)
+        for step in range(lines):
+            for half in range(HALVES):
+                copies[half, 3 * lines + step].wait_recv()
 
         loads["edge_out", layer_id].wait()
         partial_sum[...] = jnp.zeros_like(partial_sum)
@@ -245,7 +312,7 @@
         def late(tile, carry, layer_id=layer_id):
             span = pl.ds(pl.multiple_of(tile * EDGE_ROWS, EDGE_ROWS), EDGE_ROWS)
             first_out = acc[span, :] + product(
-                onehot[span, 2 * group : send_rows], table[layer_id, 2 * group : send_rows, :]
+                onehot[span, 3 * group : send_rows], table[layer_id, 3 * group : send_rows, :]
             )
             hidden = silu(first_out).astype(jnp.bfloat16)
             if layer_id == 0:
@@ -306,29 +373,6 @@
     cols = lax.axis_size("col")
     rows = lax.axis_size("row")
     lines = cols // 4
-    piece = own // HALVES
-    row_me = lax.axis_index("row")
-    col_me = lax.axis_index("col")
-    send_patch = own * cols
-    local = senders - row_me * send_patch
-    block, offset = local // own, local % own
-    line = (block // 4 - col_me // 4) % lines
-    flip_b = (block // 2 % 2) ^ (col_me // 2 % 2)
-    flip_c = (block % 2) ^ (col_me % 2)
-    half = offset // piece
-    first = jnp.where(half == 0, flip_c, flip_b)
-    second = jnp.where(half == 0, flip_b, flip_c)
-    send_slot = (
-        (second * 2 + first) * (HALVES * lines * piece)
-        + half * (lines * piece)
-        + line * piece
-        + offset % piece
-    )
-    receive_slot = (receivers // send_patch - row_me) % rows * own + receivers % own
-    ids = jnp.stack([send_slot, receive_slot], axis=1)
-    live_mask = jnp.arange(slots, dtype=jnp.int32) < edge_count[0]
-    receive_row = jnp.where(live_mask, receive_slot, -1)[None, :]
-
     send_rows, recv_rows = cols * own, rows * own
     half_type, full_type = jnp.bfloat16, jnp.float32
     vmem = pl.BlockSpec(memory_space=pltpu.VMEM)
@@ -337,7 +381,7 @@
     return pl.pallas_call(
         functools.partial(kernel, lines),
         out_shape=jax.ShapeDtypeStruct((own, width), full_type),
-        in_specs=[vmem] * 2 + [anywhere] * 6,
+        in_specs=[pl.BlockSpec(memory_space=pltpu.SMEM)] + [vmem] * 2 + [anywhere] * 6,
         out_specs=vmem,
         scratch_shapes=[
             pltpu.VMEM((own, width), full_type),
@@ -355,6 +399,7 @@
             pltpu.VMEM((layers, rows - 1, own, width), half_type),
             pltpu.VMEM((layers, rows - 1, own, width), half_type),
             pltpu.VMEM((own, width), full_type),
+            pltpu.VMEM((2, slots), full_type),
             dma((2 + 6 * layers,)),
             dma((layers, HALVES, cols)),
             dma((layers, HALVES, cols)),
@@ -366,7 +411,7 @@
         compiler_params=pltpu.CompilerParams(
             collective_id=0, has_side_effects=True, vmem_limit_bytes=60 * 1024 * 1024
         ),
-    )(ids, receive_row, node_latent, edge_latent, edge_in, edge_out, node_in, node_out)
+    )(edge_count, senders[None, :], receivers[None, :], node_latent, edge_latent, edge_in, edge_out, node_in, node_out)
 
 
 def solution(mesh):

time: 70.2 us -> 58.9 us (0.84)
  Pallas kernels: 64.2 us -> 56.4 us
  other arithmetic: 2.08 us -> 0 us
  local copies, waits for them, and re-layouts: 2.98 us -> 1.62 us
    pallas_call x1, Pallas kernels: 64.2 us -> 56.4 us  [per_device(): pl.pallas_call(functools.partial(kernel, lines), out_shape=jax.ShapeDtype...]
    another operation x1 -> x0, local copies, waits for them, and re-layouts: 1.37 us -> none  [per_device(): ids = jnp.stack([send_slot, receive_slot], axis=1)]
    select_n x1 -> x0, other arithmetic: 1.32 us -> none  [per_device(): receive_row = jnp.where(live_mask, receive_slot, -1)[None, :]]
    add x1 -> x0, other arithmetic: 0.75 us -> none  [per_device(): (second * 2 + first) * (HALVES * lines * piece) + half * (lines * piece)]
where the time goes in v2:
time: 58.9 us; the launch traced here: 58.7 us
  Pallas kernels  56.4 us (96%)
  local copies, waits for them, and re-layouts  1.62 us (3%)
  between operations  0.66 us (1%)
    pallas_call x1, Pallas kernels, per_device(): pl.pallas_call(functools.partial(kernel, lines), out_shape=jax.ShapeDtype...  56.4 us
    unnamed x1, local copies, waits for them, and re-layouts  1.62 us

profile of v2, /device:TPU:0, one launch (start us, length us, event | category | flops | bytes accessed | tf_op | source)
XLA Modules:
  0.0 58.7 jit_solution(12264636451508985108)
XLA Ops:
  0.7 56.4 %shard_map.91 = f32[96,512]{1,0:T(8,128)} custom-call(s32[1]{0:T(128)S(6)} %copy.11.count_ref, s32[1,2048]{1,0:T(1,128)} %bitcast.2, s32[1,2048]{1,0:T(1,128)} %bitcast.3, f32[96,512]{1,0:T(8,128)} %node_hbm.1, bf16[2048,512]{1,0:T(8,128)(2,1)} %edge_hbm.1, bf16[2,1536,512]{2,1,0:T(8,128)(2,1)} %edge_in_hbm.1, bf16[2,512,512]{2,1,0:T(8,128)(2,1)} %edge_out_hbm.1, ...), custom_call_target="tpu_custom_call" | custom-call | tf_op jit(solution)/shard_map/pallas_call | solution.py:381
  57.1 1.6 %copy.12 = f32[96,512]{1,0:T(8,128)} copy(f32[96,512]{1,0:T(8,128)} %shard_map.91) | data formatting | bytes 393216

commit v3 on v2

--- a/solution.py
+++ b/solution.py
@@ -327,7 +327,7 @@
             partial_sum[...] += product(scatter_hot[:, span], after_half)
             return carry
 
-        lax.fori_loop(0, tiles, late, 0)
+        lax.fori_loop(0, tiles, late, 0, unroll=True)
 
         part_copies = []
         for step in range(1, rows):

time: 58.9 us -> 58.6 us (level)
  no operation moved by 1% of the time
where the time goes in v3:
time: 58.6 us; the launch traced here: 58.4 us
  Pallas kernels  56.1 us (96%)
  local copies, waits for them, and re-layouts  1.62 us (3%)
  between operations  0.66 us (1%)
    pallas_call x1, Pallas kernels, per_device(): pl.pallas_call(functools.partial(kernel, lines), out_shape=jax.ShapeDtype...  56.1 us
    unnamed x1, local copies, waits for them, and re-layouts  1.62 us

profile of v3, /device:TPU:0, one launch (start us, length us, event | category | flops | bytes accessed | tf_op | source)
XLA Modules:
  0.0 58.4 jit_solution(16699386753762969273)
XLA Ops:
  0.7 56.1 %shard_map.91 = f32[96,512]{1,0:T(8,128)} custom-call(s32[1]{0:T(128)S(6)} %copy.11.count_ref, s32[1,2048]{1,0:T(1,128)} %bitcast.2, s32[1,2048]{1,0:T(1,128)} %bitcast.3, f32[96,512]{1,0:T(8,128)} %node_hbm.1, bf16[2048,512]{1,0:T(8,128)(2,1)} %edge_hbm.1, bf16[2,1536,512]{2,1,0:T(8,128)(2,1)} %edge_in_hbm.1, bf16[2,512,512]{2,1,0:T(8,128)(2,1)} %edge_out_hbm.1, ...), custom_call_target="tpu_custom_call" | custom-call | tf_op jit(solution)/shard_map/pallas_call | solution.py:381
  56.8 1.6 %copy.12 = f32[96,512]{1,0:T(8,128)} copy(f32[96,512]{1,0:T(8,128)} %shard_map.91) | data formatting | bytes 393216
